TPU v7x, 256 devices: a whole 4x4x8 slice. The times are simulated.
256 devices in a mesh: pipe: 8 (over y, core), hidden: 32 (over z, x).
Axes of the slice: x: 4, y: 4, z: 8, core: 2. Of those that a mesh axis runs over, the one named last changes fastest.
Arguments:
- acts: bfloat16 [8, 1024, 16384], P('pipe', None, 'hidden'), may hold values from -6 to 6
- factors: bfloat16 [8, 4, 128, 128, 128], P('pipe', None, 'hidden'), may hold values from -0.5 to 0.5
- cotangent: bfloat16 [1024, 16384], P(None, 'hidden'), may hold values from -6 to 6
Outputs:
- input_grads: bfloat16 [8, 1024, 16384], P('pipe', None, 'hidden')
- factor_grads: float32 [8, 4, 128, 128, 128], P('pipe', None, 'hidden')
All inputs are finite; a program needn't handle non-finite values.
Results may differ from a plain program's by a relative error of at most 0.03.
Values may be sent and summed in bfloat16 or wider, within the bound.
A program may use at most 64 MiB of HBM per device.

v0:
```python
import jax
import jax.numpy as jnp
from jax import lax
from jax.sharding import PartitionSpec as P


def shifted(value, axis, steps):
    count = lax.axis_size(axis)
    leading, last = (max(0, -steps), min(count, count - steps))
    return lax.ppermute(value, axis, [(source, source + steps) for source in range(leading, last)])


def gelu_slope(value):
    coeff = 0.7978845608028654
    inner = coeff * (value + 0.044715 * value**3)
    tangent = jnp.tanh(inner)
    return 0.5 * (1.0 + tangent) + 0.5 * value * (1.0 - tangent * tangent) * coeff * (
        1.0 + 3.0 * 0.044715 * value * value
    )


def forward_pair(inputs, weights, first_mixer, second_mixer):
    first_part = jnp.einsum(
        "tab,acb->act", inputs, weights[0], preferred_element_type=jnp.float32
    ).astype(jnp.bfloat16)
    mixed_one = first_mixer(first_part)
    hidden_pre = jnp.einsum(
        "act,cda->tcd", mixed_one, weights[1], preferred_element_type=jnp.float32
    )
    activ = jax.nn.gelu(hidden_pre, approximate=True).astype(jnp.bfloat16)
    second_part = jnp.einsum(
        "tab,acb->act", activ, weights[2], preferred_element_type=jnp.float32
    ).astype(jnp.bfloat16)
    mixed_two = second_mixer(second_part)
    return (hidden_pre, mixed_one, activ, mixed_two)


def grad_pair(grad_out, mixed_output, inputs, right_factor, left_factor, mixer):
    left_factor_gradient = jnp.einsum(
        "tcd,act->cda", grad_out, mixed_output, preferred_element_type=jnp.float32
    )
    mixed_gradient = jnp.einsum(
        "tcd,cda->act", grad_out, left_factor, preferred_element_type=jnp.float32
    ).astype(jnp.bfloat16)
    grad_part = mixer(mixed_gradient)
    right_factor_gradient = jnp.einsum(
        "act,tab->acb", grad_part, inputs, preferred_element_type=jnp.float32
    )
    input_gradient = jnp.einsum(
        "act,acb->tab", grad_part, right_factor, preferred_element_type=jnp.float32
    )
    return (input_gradient, right_factor_gradient, left_factor_gradient)


def shards(acts, factors, cotangent):
    weights = factors[0]
    local_blocks = weights.shape[1]
    block_size = weights.shape[2]
    total_rows = acts.shape[1]
    inputs_all = acts[0].reshape(total_rows, local_blocks, block_size)
    upstream = cotangent.reshape(total_rows, local_blocks, block_size)
    sections = lax.axis_size("pipe")
    section = lax.axis_index("pipe")
    piece_rows = total_rows // sections
    turns = sections + sections - 1
    stored = forward_pair(
        inputs_all,
        weights,
        lambda sent: lax.all_to_all(sent, "hidden", split_axis=1, concat_axis=0, tiled=True),
        lambda sent: lax.all_to_all(sent, "hidden", split_axis=1, concat_axis=0, tiled=True),
    )

    def advance(moment, carry):
        previous, grads_in, grads_fac = carry
        incoming = shifted(previous, "pipe", -1)
        piece_no = moment - (sections - 1 - section)
        active = jnp.logical_and(piece_no >= 0, piece_no < sections)
        start = jnp.clip(piece_no, 0, sections - 1) * piece_rows
        block_inputs = lax.dynamic_slice_in_dim(inputs_all, start, piece_rows, 0)
        top_grad = lax.dynamic_slice_in_dim(upstream, start, piece_rows, 0)
        grad_out = jnp.where(section == sections - 1, top_grad, incoming)
        hidden_pre = lax.dynamic_slice_in_dim(stored[0], start, piece_rows, 0)
        mixed_one = lax.dynamic_slice_in_dim(stored[1], start, piece_rows, 2)
        activ = lax.dynamic_slice_in_dim(stored[2], start, piece_rows, 0)
        mixed_two = lax.dynamic_slice_in_dim(stored[3], start, piece_rows, 2)
        grad_act, grad_r2, grad_l2 = grad_pair(
            grad_out,
            mixed_two,
            activ,
            weights[2],
            weights[3],
            lambda sent: lax.all_to_all(sent, "hidden", split_axis=0, concat_axis=1, tiled=True),
        )
        grad_hid = (grad_act * gelu_slope(hidden_pre)).astype(jnp.bfloat16)
        grad_x, grad_r1, grad_l1 = grad_pair(
            grad_hid,
            mixed_one,
            block_inputs,
            weights[0],
            weights[1],
            lambda sent: lax.all_to_all(sent, "hidden", split_axis=0, concat_axis=1, tiled=True),
        )
        block_gradient = (grad_out.astype(jnp.float32) + grad_x).astype(jnp.bfloat16)
        older = lax.dynamic_slice_in_dim(grads_in, start, piece_rows, 0)
        grads_in = lax.dynamic_update_slice_in_dim(
            grads_in, jnp.where(active, block_gradient, older), start, 0
        )
        stacked = jnp.stack([grad_r1, grad_l1, grad_r2, grad_l2])
        grads_fac = grads_fac + jnp.where(active, stacked, jnp.zeros_like(stacked))
        return (block_gradient, grads_in, grads_fac)

    initial = (
        jnp.zeros((piece_rows, local_blocks, block_size), jnp.bfloat16),
        jnp.zeros((total_rows, local_blocks, block_size), jnp.bfloat16),
        jnp.zeros((4, local_blocks, block_size, block_size), jnp.float32),
    )
    unused, grads_in, grads_fac = lax.fori_loop(0, turns, advance, initial)
    scale = total_rows ** (-0.5)
    return (grads_in.reshape(1, total_rows, local_blocks * block_size), (grads_fac * scale)[None])


def solution(mesh):
    in_specs = (P("pipe", None, "hidden"), P("pipe", None, "hidden", None, None), P(None, "hidden"))
    out_specs = (P("pipe", None, "hidden"), P("pipe", None, "hidden", None, None))
    return jax.shard_map(shards, mesh=mesh, in_specs=in_specs, out_specs=out_specs, check_vma=False)
```

profile of v0, /device:TPU:2, one launch (start us, length us, event | category | flops | bytes accessed | tf_op | source)
XLA Modules:
  0.0 681.1 jit_solution(1797412314697735468)
XLA Ops:
  3.5 39.5 %all_to_all.124 = bf16[4,128,1024]{2,0,1:T(4,128)(2,1)S(1)} all-to-all(bf16[4,128,1024]{2,0,1:T(4,128)(2,1)S(1)} %copy.66), channel_id=1, replica_groups=mesh['pipe'=8,'hidden'=32] {'hidden'}, dimensions={1} | all-to-all | bytes 2097152 | tf_op jit(solution)/shard_map/all_to_all | solution.py:69
  49.0 5.6 all-to-all-start.3
  56.9 24.7 %all-to-all-done.3 = bf16[4,128,1024]{2,0,1:T(4,128)(2,1)S(1)} async-done(((bf16[4,128,1024]{2,0,1:T(4,128)(2,1)}), bf16[4,128,1024]{2,0,1:T(4,128)(2,1)S(1)}, u32[]{:S(2)}, u32[]{:S(2)}) %all-to-all-start.3) | async-done | bytes 1048608 | tf_op jit(solution)/shard_map/all_to_all | solution.py:70
  84.4 593.4 %while.20 = (s32[]{:T(128)}, bf16[128,4,128]{2,0,1:T(8,128)(2,1)S(1)}, bf16[1024,4,128]{2,1,0:T(4,128)(2,1)}, f32[4,4,128,128]{3,2,1,0:T(8,128)S(1)}, pred[]{:T(...) while((s32[]{:T(128)}, ...), condition=%wide.region_1.2_spmd.clone, body=%wide.region_0.1_spmd.clone.sunk | while | flops 137560080 | bytes 12583334 | solution.py:117
  88.6 5.6 all-to-all-start
  96.2 6.9 %all-to-all-done = bf16[128,4,128]{2,1,0:T(4,128)(2,1)S(1)} async-done(((bf16[128,4,128]{2,1,0:T(4,128)(2,1)}), bf16[128,4,128]{2,1,0:T(4,128)(2,1)S(1)}, u32[]{:S(2)}, u32[]{:S(2)}) %all-to-all-start) | async-done | bytes 131104 | tf_op jit(solution)/shard_map/while/body/eval_jaxpr/all_to_all | solution.py:92
  112.3 7.5 %all-to-all-done.1 = bf16[128,4,128]{2,1,0:T(4,128)(2,1)S(1)} async-done(((bf16[128,4,128]{2,1,0:T(4,128)(2,1)}), bf16[128,4,128]{2,1,0:T(4,128)(2,1)S(1)}, u32[]{:S(2)}, u32[]{:S(2)}) %all-to-all-start.1) | async-done | bytes 131104 | tf_op jit(solution)/shard_map/while/body/eval_jaxpr/all_to_all | solution.py:101
  127.1 5.7 all-to-all-start
  134.9 6.9 %all-to-all-done = bf16[128,4,128]{2,1,0:T(4,128)(2,1)S(1)} async-done(((bf16[128,4,128]{2,1,0:T(4,128)(2,1)}), bf16[128,4,128]{2,1,0:T(4,128)(2,1)S(1)}, u32[]{:S(2)}, u32[]{:S(2)}) %all-to-all-start) | async-done | bytes 131104 | tf_op jit(solution)/shard_map/while/body/eval_jaxpr/all_to_all | solution.py:92
  144.1 5.5 all-to-all-start.1
  151.1 7.4 %all-to-all-done.1 = bf16[128,4,128]{2,1,0:T(4,128)(2,1)S(1)} async-done(((bf16[128,4,128]{2,1,0:T(4,128)(2,1)}), bf16[128,4,128]{2,1,0:T(4,128)(2,1)S(1)}, u32[]{:S(2)}, u32[]{:S(2)}) %all-to-all-start.1) | async-done | bytes 131104 | tf_op jit(solution)/shard_map/while/body/eval_jaxpr/all_to_all | solution.py:101
  175.2 6.9 %all-to-all-done = bf16[128,4,128]{2,1,0:T(4,128)(2,1)S(1)} async-done(((bf16[128,4,128]{2,1,0:T(4,128)(2,1)}), bf16[128,4,128]{2,1,0:T(4,128)(2,1)S(1)}, u32[]{:S(2)}, u32[]{:S(2)}) %all-to-all-start) | async-done | bytes 131104 | tf_op jit(solution)/shard_map/while/body/eval_jaxpr/all_to_all | solution.py:92
  184.4 5.5 all-to-all-start.1
  191.5 7.4 %all-to-all-done.1 = bf16[128,4,128]{2,1,0:T(4,128)(2,1)S(1)} async-done(((bf16[128,4,128]{2,1,0:T(4,128)(2,1)}), bf16[128,4,128]{2,1,0:T(4,128)(2,1)S(1)}, u32[]{:S(2)}, u32[]{:S(2)}) %all-to-all-start.1) | async-done | bytes 131104 | tf_op jit(solution)/shard_map/while/body/eval_jaxpr/all_to_all | solution.py:101
  208.1 5.5 all-to-all-start
  215.6 6.9 %all-to-all-done = bf16[128,4,128]{2,1,0:T(4,128)(2,1)S(1)} async-done(((bf16[128,4,128]{2,1,0:T(4,128)(2,1)}), bf16[128,4,128]{2,1,0:T(4,128)(2,1)S(1)}, u32[]{:S(2)}, u32[]{:S(2)}) %all-to-all-start) | async-done | bytes 131104 | tf_op jit(solution)/shard_map/while/body/eval_jaxpr/all_to_all | solution.py:92
  224.9 5.5 all-to-all-start.1
  231.9 7.4 %all-to-all-done.1 = bf16[128,4,128]{2,1,0:T(4,128)(2,1)S(1)} async-done(((bf16[128,4,128]{2,1,0:T(4,128)(2,1)}), bf16[128,4,128]{2,1,0:T(4,128)(2,1)S(1)}, u32[]{:S(2)}, u32[]{:S(2)}) %all-to-all-start.1) | async-done | bytes 131104 | tf_op jit(solution)/shard_map/while/body/eval_jaxpr/all_to_all | solution.py:101
  248.9 5.5 all-to-all-start
  256.4 6.9 %all-to-all-done = bf16[128,4,128]{2,1,0:T(4,128)(2,1)S(1)} async-done(((bf16[128,4,128]{2,1,0:T(4,128)(2,1)}), bf16[128,4,128]{2,1,0:T(4,128)(2,1)S(1)}, u32[]{:S(2)}, u32[]{:S(2)}) %all-to-all-start) | async-done | bytes 131104 | tf_op jit(solution)/shard_map/while/body/eval_jaxpr/all_to_all | solution.py:92
  265.7 5.5 all-to-all-start.1
  272.7 7.4 %all-to-all-done.1 = bf16[128,4,128]{2,1,0:T(4,128)(2,1)S(1)} async-done(((bf16[128,4,128]{2,1,0:T(4,128)(2,1)}), bf16[128,4,128]{2,1,0:T(4,128)(2,1)S(1)}, u32[]{:S(2)}, u32[]{:S(2)}) %all-to-all-start.1) | async-done | bytes 131104 | tf_op jit(solution)/shard_map/while/body/eval_jaxpr/all_to_all | solution.py:101
  289.6 5.5 all-to-all-start
  297.2 6.9 %all-to-all-done = bf16[128,4,128]{2,1,0:T(4,128)(2,1)S(1)} async-done(((bf16[128,4,128]{2,1,0:T(4,128)(2,1)}), bf16[128,4,128]{2,1,0:T(4,128)(2,1)S(1)}, u32[]{:S(2)}, u32[]{:S(2)}) %all-to-all-start) | async-done | bytes 131104 | tf_op jit(solution)/shard_map/while/body/eval_jaxpr/all_to_all | solution.py:92
  306.4 5.5 all-to-all-start.1
  313.5 7.4 %all-to-all-done.1 = bf16[128,4,128]{2,1,0:T(4,128)(2,1)S(1)} async-done(((bf16[128,4,128]{2,1,0:T(4,128)(2,1)}), bf16[128,4,128]{2,1,0:T(4,128)(2,1)S(1)}, u32[]{:S(2)}, u32[]{:S(2)}) %all-to-all-start.1) | async-done | bytes 131104 | tf_op jit(solution)/shard_map/while/body/eval_jaxpr/all_to_all | solution.py:101
  329.6 5.5 all-to-all-start
  337.1 6.9 %all-to-all-done = bf16[128,4,128]{2,1,0:T(4,128)(2,1)S(1)} async-done(((bf16[128,4,128]{2,1,0:T(4,128)(2,1)}), bf16[128,4,128]{2,1,0:T(4,128)(2,1)S(1)}, u32[]{:S(2)}, u32[]{:S(2)}) %all-to-all-start) | async-done | bytes 131104 | tf_op jit(solution)/shard_map/while/body/eval_jaxpr/all_to_all | solution.py:92
  346.3 5.5 all-to-all-start.1
  353.4 7.4 %all-to-all-done.1 = bf16[128,4,128]{2,1,0:T(4,128)(2,1)S(1)} async-done(((bf16[128,4,128]{2,1,0:T(4,128)(2,1)}), bf16[128,4,128]{2,1,0:T(4,128)(2,1)S(1)}, u32[]{:S(2)}, u32[]{:S(2)}) %all-to-all-start.1) | async-done | bytes 131104 | tf_op jit(solution)/shard_map/while/body/eval_jaxpr/all_to_all | solution.py:101
  376.6 6.9 %all-to-all-done = bf16[128,4,128]{2,1,0:T(4,128)(2,1)S(1)} async-done(((bf16[128,4,128]{2,1,0:T(4,128)(2,1)}), bf16[128,4,128]{2,1,0:T(4,128)(2,1)S(1)}, u32[]{:S(2)}, u32[]{:S(2)}) %all-to-all-start) | async-done | bytes 131104 | tf_op jit(solution)/shard_map/while/body/eval_jaxpr/all_to_all | solution.py:92
  385.8 5.5 all-to-all-start.1
  392.9 7.4 %all-to-all-done.1 = bf16[128,4,128]{2,1,0:T(4,128)(2,1)S(1)} async-done(((bf16[128,4,128]{2,1,0:T(4,128)(2,1)}), bf16[128,4,128]{2,1,0:T(4,128)(2,1)S(1)}, u32[]{:S(2)}, u32[]{:S(2)}) %all-to-all-start.1) | async-done | bytes 131104 | tf_op jit(solution)/shard_map/while/body/eval_jaxpr/all_to_all | solution.py:101
  415.9 6.9 %all-to-all-done = bf16[128,4,128]{2,1,0:T(4,128)(2,1)S(1)} async-done(((bf16[128,4,128]{2,1,0:T(4,128)(2,1)}), bf16[128,4,128]{2,1,0:T(4,128)(2,1)S(1)}, u32[]{:S(2)}, u32[]{:S(2)}) %all-to-all-start) | async-done | bytes 131104 | tf_op jit(solution)/shard_map/while/body/eval_jaxpr/all_to_all | solution.py:92
  425.1 5.5 all-to-all-start.1
  432.1 7.4 %all-to-all-done.1 = bf16[128,4,128]{2,1,0:T(4,128)(2,1)S(1)} async-done(((bf16[128,4,128]{2,1,0:T(4,128)(2,1)}), bf16[128,4,128]{2,1,0:T(4,128)(2,1)S(1)}, u32[]{:S(2)}, u32[]{:S(2)}) %all-to-all-start.1) | async-done | bytes 131104 | tf_op jit(solution)/shard_map/while/body/eval_jaxpr/all_to_all | solution.py:101
  455.1 6.9 %all-to-all-done = bf16[128,4,128]{2,1,0:T(4,128)(2,1)S(1)} async-done(((bf16[128,4,128]{2,1,0:T(4,128)(2,1)}), bf16[128,4,128]{2,1,0:T(4,128)(2,1)S(1)}, u32[]{:S(2)}, u32[]{:S(2)}) %all-to-all-start) | async-done | bytes 131104 | tf_op jit(solution)/shard_map/while/body/eval_jaxpr/all_to_all | solution.py:92
  471.4 7.4 %all-to-all-done.1 = bf16[128,4,128]{2,1,0:T(4,128)(2,1)S(1)} async-done(((bf16[128,4,128]{2,1,0:T(4,128)(2,1)}), bf16[128,4,128]{2,1,0:T(4,128)(2,1)S(1)}, u32[]{:S(2)}, u32[]{:S(2)}) %all-to-all-start.1) | async-done | bytes 131104 | tf_op jit(solution)/shard_map/while/body/eval_jaxpr/all_to_all | solution.py:101
  494.4 6.9 %all-to-all-done = bf16[128,4,128]{2,1,0:T(4,128)(2,1)S(1)} async-done(((bf16[128,4,128]{2,1,0:T(4,128)(2,1)}), bf16[128,4,128]{2,1,0:T(4,128)(2,1)S(1)}, u32[]{:S(2)}, u32[]{:S(2)}) %all-to-all-start) | async-done | bytes 131104 | tf_op jit(solution)/shard_map/while/body/eval_jaxpr/all_to_all | solution.py:92
  510.7 7.4 %all-to-all-done.1 = bf16[128,4,128]{2,1,0:T(4,128)(2,1)S(1)} async-done(((bf16[128,4,128]{2,1,0:T(4,128)(2,1)}), bf16[128,4,128]{2,1,0:T(4,128)(2,1)S(1)}, u32[]{:S(2)}, u32[]{:S(2)}) %all-to-all-start.1) | async-done | bytes 131104 | tf_op jit(solution)/shard_map/while/body/eval_jaxpr/all_to_all | solution.py:101
  533.7 6.9 %all-to-all-done = bf16[128,4,128]{2,1,0:T(4,128)(2,1)S(1)} async-done(((bf16[128,4,128]{2,1,0:T(4,128)(2,1)}), bf16[128,4,128]{2,1,0:T(4,128)(2,1)S(1)}, u32[]{:S(2)}, u32[]{:S(2)}) %all-to-all-start) | async-done | bytes 131104 | tf_op jit(solution)/shard_map/while/body/eval_jaxpr/all_to_all | solution.py:92
  549.9 7.4 %all-to-all-done.1 = bf16[128,4,128]{2,1,0:T(4,128)(2,1)S(1)} async-done(((bf16[128,4,128]{2,1,0:T(4,128)(2,1)}), bf16[128,4,128]{2,1,0:T(4,128)(2,1)S(1)}, u32[]{:S(2)}, u32[]{:S(2)}) %all-to-all-start.1) | async-done | bytes 131104 | tf_op jit(solution)/shard_map/while/body/eval_jaxpr/all_to_all | solution.py:101
  572.9 6.9 %all-to-all-done = bf16[128,4,128]{2,1,0:T(4,128)(2,1)S(1)} async-done(((bf16[128,4,128]{2,1,0:T(4,128)(2,1)}), bf16[128,4,128]{2,1,0:T(4,128)(2,1)S(1)}, u32[]{:S(2)}, u32[]{:S(2)}) %all-to-all-start) | async-done | bytes 131104 | tf_op jit(solution)/shard_map/while/body/eval_jaxpr/all_to_all | solution.py:92
  589.2 7.4 %all-to-all-done.1 = bf16[128,4,128]{2,1,0:T(4,128)(2,1)S(1)} async-done(((bf16[128,4,128]{2,1,0:T(4,128)(2,1)}), bf16[128,4,128]{2,1,0:T(4,128)(2,1)S(1)}, u32[]{:S(2)}, u32[]{:S(2)}) %all-to-all-start.1) | async-done | bytes 131104 | tf_op jit(solution)/shard_map/while/body/eval_jaxpr/all_to_all | solution.py:101
  612.2 6.9 %all-to-all-done = bf16[128,4,128]{2,1,0:T(4,128)(2,1)S(1)} async-done(((bf16[128,4,128]{2,1,0:T(4,128)(2,1)}), bf16[128,4,128]{2,1,0:T(4,128)(2,1)S(1)}, u32[]{:S(2)}, u32[]{:S(2)}) %all-to-all-start) | async-done | bytes 131104 | tf_op jit(solution)/shard_map/while/body/eval_jaxpr/all_to_all | solution.py:92
  628.5 7.4 %all-to-all-done.1 = bf16[128,4,128]{2,1,0:T(4,128)(2,1)S(1)} async-done(((bf16[128,4,128]{2,1,0:T(4,128)(2,1)}), bf16[128,4,128]{2,1,0:T(4,128)(2,1)S(1)}, u32[]{:S(2)}, u32[]{:S(2)}) %all-to-all-start.1) | async-done | bytes 131104 | tf_op jit(solution)/shard_map/while/body/eval_jaxpr/all_to_all | solution.py:101
  651.5 6.9 %all-to-all-done = bf16[128,4,128]{2,1,0:T(4,128)(2,1)S(1)} async-done(((bf16[128,4,128]{2,1,0:T(4,128)(2,1)}), bf16[128,4,128]{2,1,0:T(4,128)(2,1)S(1)}, u32[]{:S(2)}, u32[]{:S(2)}) %all-to-all-start) | async-done | bytes 131104 | tf_op jit(solution)/shard_map/while/body/eval_jaxpr/all_to_all | solution.py:92
  667.7 7.4 %all-to-all-done.1 = bf16[128,4,128]{2,1,0:T(4,128)(2,1)S(1)} async-done(((bf16[128,4,128]{2,1,0:T(4,128)(2,1)}), bf16[128,4,128]{2,1,0:T(4,128)(2,1)S(1)}, u32[]{:S(2)}, u32[]{:S(2)}) %all-to-all-start.1) | async-done | bytes 131104 | tf_op jit(solution)/shard_map/while/body/eval_jaxpr/all_to_all | solution.py:101
  (398 shorter events, 316.8 us)
Async XLA Ops:
  0.6 1.6 copy-start
  43.5 2.4 copy-start.2
  49.0 32.6 %all-to-all-start.3 = ((bf16[4,128,1024]{2,0,1:T(4,128)(2,1)}), bf16[4,128,1024]{2,0,1:T(4,128)(2,1)S(1)}, u32[]{:S(2)}, u32[]{:S(2)}) async-start(bf16[4,128,1024]{2,0,1:T(4,128)(2,1)} %copy.69), calls=%async_computation.3 | async-start | bytes 2097152 | tf_op jit(solution)/shard_map/all_to_all | solution.py:70
  84.4 3.2 collective-permute-start
  88.6 14.5 %all-to-all-start = ((bf16[128,4,128]{2,1,0:T(4,128)(2,1)}), bf16[128,4,128]{2,1,0:T(4,128)(2,1)S(1)}, u32[]{:S(2)}, u32[]{:S(2)}) async-start(bf16[128,4,128]{2,1,0:T(4,128)(2,1)} %copy.114), calls=%async_computation | async-start | bytes 262144 | tf_op jit(solution)/shard_map/while/body/eval_jaxpr/all_to_all | solution.py:92
  105.4 14.4 %all-to-all-start.1 = ((bf16[128,4,128]{2,1,0:T(4,128)(2,1)}), bf16[128,4,128]{2,1,0:T(4,128)(2,1)S(1)}, u32[]{:S(2)}, u32[]{:S(2)}) async-start(bf16[128,4,128]{2,1,0:T(4,128)(2,1)} %copy.117), calls=%async_computation.1 | async-start | bytes 262144 | tf_op jit(solution)/shard_map/while/body/eval_jaxpr/all_to_all | solution.py:101
  122.5 3.6 collective-permute-start
  127.1 14.7 %all-to-all-start = ((bf16[128,4,128]{2,1,0:T(4,128)(2,1)}), bf16[128,4,128]{2,1,0:T(4,128)(2,1)S(1)}, u32[]{:S(2)}, u32[]{:S(2)}) async-start(bf16[128,4,128]{2,1,0:T(4,128)(2,1)} %copy.114), calls=%async_computation | async-start | bytes 262144 | tf_op jit(solution)/shard_map/while/body/eval_jaxpr/all_to_all | solution.py:92
  144.1 14.5 %all-to-all-start.1 = ((bf16[128,4,128]{2,1,0:T(4,128)(2,1)}), bf16[128,4,128]{2,1,0:T(4,128)(2,1)S(1)}, u32[]{:S(2)}, u32[]{:S(2)}) async-start(bf16[128,4,128]{2,1,0:T(4,128)(2,1)} %copy.117), calls=%async_computation.1 | async-start | bytes 262144 | tf_op jit(solution)/shard_map/while/body/eval_jaxpr/all_to_all | solution.py:101
  161.3 5.5 collective-permute-start
  167.7 14.4 %all-to-all-start = ((bf16[128,4,128]{2,1,0:T(4,128)(2,1)}), bf16[128,4,128]{2,1,0:T(4,128)(2,1)S(1)}, u32[]{:S(2)}, u32[]{:S(2)}) async-start(bf16[128,4,128]{2,1,0:T(4,128)(2,1)} %copy.114), calls=%async_computation | async-start | bytes 262144 | tf_op jit(solution)/shard_map/while/body/eval_jaxpr/all_to_all | solution.py:92
  184.4 14.4 %all-to-all-start.1 = ((bf16[128,4,128]{2,1,0:T(4,128)(2,1)}), bf16[128,4,128]{2,1,0:T(4,128)(2,1)S(1)}, u32[]{:S(2)}, u32[]{:S(2)}) async-start(bf16[128,4,128]{2,1,0:T(4,128)(2,1)} %copy.117), calls=%async_computation.1 | async-start | bytes 262144 | tf_op jit(solution)/shard_map/while/body/eval_jaxpr/all_to_all | solution.py:101
  201.5 5.6 collective-permute-start
  208.1 14.4 %all-to-all-start = ((bf16[128,4,128]{2,1,0:T(4,128)(2,1)}), bf16[128,4,128]{2,1,0:T(4,128)(2,1)S(1)}, u32[]{:S(2)}, u32[]{:S(2)}) async-start(bf16[128,4,128]{2,1,0:T(4,128)(2,1)} %copy.114), calls=%async_computation | async-start | bytes 262144 | tf_op jit(solution)/shard_map/while/body/eval_jaxpr/all_to_all | solution.py:92
  224.9 14.4 %all-to-all-start.1 = ((bf16[128,4,128]{2,1,0:T(4,128)(2,1)}), bf16[128,4,128]{2,1,0:T(4,128)(2,1)S(1)}, u32[]{:S(2)}, u32[]{:S(2)}) async-start(bf16[128,4,128]{2,1,0:T(4,128)(2,1)} %copy.117), calls=%async_computation.1 | async-start | bytes 262144 | tf_op jit(solution)/shard_map/while/body/eval_jaxpr/all_to_all | solution.py:101
  242.0 6.0 collective-permute-start
  248.9 14.4 %all-to-all-start = ((bf16[128,4,128]{2,1,0:T(4,128)(2,1)}), bf16[128,4,128]{2,1,0:T(4,128)(2,1)S(1)}, u32[]{:S(2)}, u32[]{:S(2)}) async-start(bf16[128,4,128]{2,1,0:T(4,128)(2,1)} %copy.114), calls=%async_computation | async-start | bytes 262144 | tf_op jit(solution)/shard_map/while/body/eval_jaxpr/all_to_all | solution.py:92
  265.7 14.4 %all-to-all-start.1 = ((bf16[128,4,128]{2,1,0:T(4,128)(2,1)}), bf16[128,4,128]{2,1,0:T(4,128)(2,1)S(1)}, u32[]{:S(2)}, u32[]{:S(2)}) async-start(bf16[128,4,128]{2,1,0:T(4,128)(2,1)} %copy.117), calls=%async_computation.1 | async-start | bytes 262144 | tf_op jit(solution)/shard_map/while/body/eval_jaxpr/all_to_all | solution.py:101
  282.8 5.9 collective-permute-start
  289.6 14.5 %all-to-all-start = ((bf16[128,4,128]{2,1,0:T(4,128)(2,1)}), bf16[128,4,128]{2,1,0:T(4,128)(2,1)S(1)}, u32[]{:S(2)}, u32[]{:S(2)}) async-start(bf16[128,4,128]{2,1,0:T(4,128)(2,1)} %copy.114), calls=%async_computation | async-start | bytes 262144 | tf_op jit(solution)/shard_map/while/body/eval_jaxpr/all_to_all | solution.py:92
  306.4 14.4 %all-to-all-start.1 = ((bf16[128,4,128]{2,1,0:T(4,128)(2,1)}), bf16[128,4,128]{2,1,0:T(4,128)(2,1)S(1)}, u32[]{:S(2)}, u32[]{:S(2)}) async-start(bf16[128,4,128]{2,1,0:T(4,128)(2,1)} %copy.117), calls=%async_computation.1 | async-start | bytes 262144 | tf_op jit(solution)/shard_map/while/body/eval_jaxpr/all_to_all | solution.py:101
  323.5 5.1 collective-permute-start
  329.6 14.4 %all-to-all-start = ((bf16[128,4,128]{2,1,0:T(4,128)(2,1)}), bf16[128,4,128]{2,1,0:T(4,128)(2,1)S(1)}, u32[]{:S(2)}, u32[]{:S(2)}) async-start(bf16[128,4,128]{2,1,0:T(4,128)(2,1)} %copy.114), calls=%async_computation | async-start | bytes 262144 | tf_op jit(solution)/shard_map/while/body/eval_jaxpr/all_to_all | solution.py:92
  346.3 14.4 %all-to-all-start.1 = ((bf16[128,4,128]{2,1,0:T(4,128)(2,1)}), bf16[128,4,128]{2,1,0:T(4,128)(2,1)S(1)}, u32[]{:S(2)}, u32[]{:S(2)}) async-start(bf16[128,4,128]{2,1,0:T(4,128)(2,1)} %copy.117), calls=%async_computation.1 | async-start | bytes 262144 | tf_op jit(solution)/shard_map/while/body/eval_jaxpr/all_to_all | solution.py:101
  363.5 4.7 collective-permute-start
  369.2 14.3 %all-to-all-start = ((bf16[128,4,128]{2,1,0:T(4,128)(2,1)}), bf16[128,4,128]{2,1,0:T(4,128)(2,1)S(1)}, u32[]{:S(2)}, u32[]{:S(2)}) async-start(bf16[128,4,128]{2,1,0:T(4,128)(2,1)} %copy.114), calls=%async_computation | async-start | bytes 262144 | tf_op jit(solution)/shard_map/while/body/eval_jaxpr/all_to_all | solution.py:92
  385.8 14.4 %all-to-all-start.1 = ((bf16[128,4,128]{2,1,0:T(4,128)(2,1)}), bf16[128,4,128]{2,1,0:T(4,128)(2,1)S(1)}, u32[]{:S(2)}, u32[]{:S(2)}) async-start(bf16[128,4,128]{2,1,0:T(4,128)(2,1)} %copy.117), calls=%async_computation.1 | async-start | bytes 262144 | tf_op jit(solution)/shard_map/while/body/eval_jaxpr/all_to_all | solution.py:101
  403.0 4.4 collective-permute-start
  408.3 14.4 %all-to-all-start = ((bf16[128,4,128]{2,1,0:T(4,128)(2,1)}), bf16[128,4,128]{2,1,0:T(4,128)(2,1)S(1)}, u32[]{:S(2)}, u32[]{:S(2)}) async-start(bf16[128,4,128]{2,1,0:T(4,128)(2,1)} %copy.114), calls=%async_computation | async-start | bytes 262144 | tf_op jit(solution)/shard_map/while/body/eval_jaxpr/all_to_all | solution.py:92
  425.1 14.4 %all-to-all-start.1 = ((bf16[128,4,128]{2,1,0:T(4,128)(2,1)}), bf16[128,4,128]{2,1,0:T(4,128)(2,1)S(1)}, u32[]{:S(2)}, u32[]{:S(2)}) async-start(bf16[128,4,128]{2,1,0:T(4,128)(2,1)} %copy.117), calls=%async_computation.1 | async-start | bytes 262144 | tf_op jit(solution)/shard_map/while/body/eval_jaxpr/all_to_all | solution.py:101
  442.2 4.4 collective-permute-start
  447.6 14.4 %all-to-all-start = ((bf16[128,4,128]{2,1,0:T(4,128)(2,1)}), bf16[128,4,128]{2,1,0:T(4,128)(2,1)S(1)}, u32[]{:S(2)}, u32[]{:S(2)}) async-start(bf16[128,4,128]{2,1,0:T(4,128)(2,1)} %copy.114), calls=%async_computation | async-start | bytes 262144 | tf_op jit(solution)/shard_map/while/body/eval_jaxpr/all_to_all | solution.py:92
  464.4 14.4 %all-to-all-start.1 = ((bf16[128,4,128]{2,1,0:T(4,128)(2,1)}), bf16[128,4,128]{2,1,0:T(4,128)(2,1)S(1)}, u32[]{:S(2)}, u32[]{:S(2)}) async-start(bf16[128,4,128]{2,1,0:T(4,128)(2,1)} %copy.117), calls=%async_computation.1 | async-start | bytes 262144 | tf_op jit(solution)/shard_map/while/body/eval_jaxpr/all_to_all | solution.py:101
  481.5 4.4 collective-permute-start
  486.9 14.4 %all-to-all-start = ((bf16[128,4,128]{2,1,0:T(4,128)(2,1)}), bf16[128,4,128]{2,1,0:T(4,128)(2,1)S(1)}, u32[]{:S(2)}, u32[]{:S(2)}) async-start(bf16[128,4,128]{2,1,0:T(4,128)(2,1)} %copy.114), calls=%async_computation | async-start | bytes 262144 | tf_op jit(solution)/shard_map/while/body/eval_jaxpr/all_to_all | solution.py:92
  503.6 14.4 %all-to-all-start.1 = ((bf16[128,4,128]{2,1,0:T(4,128)(2,1)}), bf16[128,4,128]{2,1,0:T(4,128)(2,1)S(1)}, u32[]{:S(2)}, u32[]{:S(2)}) async-start(bf16[128,4,128]{2,1,0:T(4,128)(2,1)} %copy.117), calls=%async_computation.1 | async-start | bytes 262144 | tf_op jit(solution)/shard_map/while/body/eval_jaxpr/all_to_all | solution.py:101
  520.7 4.4 collective-permute-start
  526.1 14.4 %all-to-all-start = ((bf16[128,4,128]{2,1,0:T(4,128)(2,1)}), bf16[128,4,128]{2,1,0:T(4,128)(2,1)S(1)}, u32[]{:S(2)}, u32[]{:S(2)}) async-start(bf16[128,4,128]{2,1,0:T(4,128)(2,1)} %copy.114), calls=%async_computation | async-start | bytes 262144 | tf_op jit(solution)/shard_map/while/body/eval_jaxpr/all_to_all | solution.py:92
  542.9 14.4 %all-to-all-start.1 = ((bf16[128,4,128]{2,1,0:T(4,128)(2,1)}), bf16[128,4,128]{2,1,0:T(4,128)(2,1)S(1)}, u32[]{:S(2)}, u32[]{:S(2)}) async-start(bf16[128,4,128]{2,1,0:T(4,128)(2,1)} %copy.117), calls=%async_computation.1 | async-start | bytes 262144 | tf_op jit(solution)/shard_map/while/body/eval_jaxpr/all_to_all | solution.py:101
  560.0 4.4 collective-permute-start
  565.4 14.4 %all-to-all-start = ((bf16[128,4,128]{2,1,0:T(4,128)(2,1)}), bf16[128,4,128]{2,1,0:T(4,128)(2,1)S(1)}, u32[]{:S(2)}, u32[]{:S(2)}) async-start(bf16[128,4,128]{2,1,0:T(4,128)(2,1)} %copy.114), calls=%async_computation | async-start | bytes 262144 | tf_op jit(solution)/shard_map/while/body/eval_jaxpr/all_to_all | solution.py:92
  582.2 14.4 %all-to-all-start.1 = ((bf16[128,4,128]{2,1,0:T(4,128)(2,1)}), bf16[128,4,128]{2,1,0:T(4,128)(2,1)S(1)}, u32[]{:S(2)}, u32[]{:S(2)}) async-start(bf16[128,4,128]{2,1,0:T(4,128)(2,1)} %copy.117), calls=%async_computation.1 | async-start | bytes 262144 | tf_op jit(solution)/shard_map/while/body/eval_jaxpr/all_to_all | solution.py:101
  599.3 4.4 collective-permute-start
  604.7 14.4 %all-to-all-start = ((bf16[128,4,128]{2,1,0:T(4,128)(2,1)}), bf16[128,4,128]{2,1,0:T(4,128)(2,1)S(1)}, u32[]{:S(2)}, u32[]{:S(2)}) async-start(bf16[128,4,128]{2,1,0:T(4,128)(2,1)} %copy.114), calls=%async_computation | async-start | bytes 262144 | tf_op jit(solution)/shard_map/while/body/eval_jaxpr/all_to_all | solution.py:92
  621.4 14.4 %all-to-all-start.1 = ((bf16[128,4,128]{2,1,0:T(4,128)(2,1)}), bf16[128,4,128]{2,1,0:T(4,128)(2,1)S(1)}, u32[]{:S(2)}, u32[]{:S(2)}) async-start(bf16[128,4,128]{2,1,0:T(4,128)(2,1)} %copy.117), calls=%async_computation.1 | async-start | bytes 262144 | tf_op jit(solution)/shard_map/while/body/eval_jaxpr/all_to_all | solution.py:101
  638.5 4.4 collective-permute-start
  643.9 14.4 %all-to-all-start = ((bf16[128,4,128]{2,1,0:T(4,128)(2,1)}), bf16[128,4,128]{2,1,0:T(4,128)(2,1)S(1)}, u32[]{:S(2)}, u32[]{:S(2)}) async-start(bf16[128,4,128]{2,1,0:T(4,128)(2,1)} %copy.114), calls=%async_computation | async-start | bytes 262144 | tf_op jit(solution)/shard_map/while/body/eval_jaxpr/all_to_all | solution.py:92
  660.7 14.4 %all-to-all-start.1 = ((bf16[128,4,128]{2,1,0:T(4,128)(2,1)}), bf16[128,4,128]{2,1,0:T(4,128)(2,1)S(1)}, u32[]{:S(2)}, u32[]{:S(2)}) async-start(bf16[128,4,128]{2,1,0:T(4,128)(2,1)} %copy.117), calls=%async_computation.1 | async-start | bytes 262144 | tf_op jit(solution)/shard_map/while/body/eval_jaxpr/all_to_all | solution.py:101
  (2 other events, 2.2 us)
where the time goes:
time: 690 us; the launch traced here: 681 us
  waiting for transfers between devices  274 us (40%)
  starting transfers between devices  189 us (27%)
  local copies, waits for them, and re-layouts  97.5 us (14%)
  matrix products  70.8 us (10%)
  blocking collectives  39.5 us (6%)
  other arithmetic  7.06 us (1%)
    all_to_all x30, waiting for transfers between devices, advance(): lax.all_to_all(sent, 'hidden', split_axis=0, concat_axis=1, tiled=True)  214 us
    all_to_all x30, starting transfers between devices, advance(): lax.all_to_all(sent, 'hidden', split_axis=0, concat_axis=1, tiled=True)  164 us
    all_to_all x1, blocking collectives, shards(): lax.all_to_all(sent, 'hidden', split_axis=1, concat_axis=0, tiled=True)  39.5 us
    ppermute x15, waiting for transfers between devices, shifted(): lax.ppermute(value, axis, [(source, source + steps) for source in range(l...  34.9 us
    dot_general x30, matrix products, grad_pair(): jnp.einsum('act,tab->acb', grad_part, inputs, preferred_element_type=jnp....  32.9 us
    all_to_all x1, waiting for transfers between devices, shards(): lax.all_to_all(sent, 'hidden', split_axis=1, concat_axis=0, tiled=True)  24.7 us
    convert_element_type x30, local copies, waits for them, and re-layouts, grad_pair(): mixed_gradient = jnp.einsum('tcd,cda->act', grad_out, left_factor, prefer...  23.2 us
    dot_general x30, matrix products, grad_pair(): jnp.einsum('act,acb->tab', grad_part, right_factor, preferred_element_typ...  22.5 us
  transfers between devices with their start and end apart: 46, of which 46 were waited for; matrix products, arithmetic and copies ran while one was open for 11% of the time, Pallas kernels for 0%

commit v1 on v0

v1 whole, which is shorter than its diff:
```python
import jax
import jax.numpy as jnp
from jax import lax
from jax.experimental import pallas as pl
from jax.experimental.pallas import tpu as pltpu
from jax.sharding import PartitionSpec as P

MESH = pl.DeviceIdType.MESH
BF = jnp.bfloat16
F32 = jnp.float32
N = 128
OWN = 4
FEAT = OWN * N
LAYERS = 8
PEERS = 32
PIECE = OWN * OWN
R1, L1, R2, L2 = 0, 1, 2, 3
U1, U2, D1, D2 = 0, 1, 2, 3
HALF = FEAT // 2


def dot(a, b, ca, cb):
    return lax.dot_general(a, b, (((ca,), (cb,)), ((), ())), preferred_element_type=F32)


def blk(i, size=N):
    return pl.ds(i * size, size)


def kernel(
    acts, factors, cot, gin, gfac,
    fac, wts, xs, gs, send, recv, st, vu1, vd2, vd1, vu2, act, slope, dh, pg, px, hs, home, fin,
    lsem, a_s, a_r, w_s, w_r, f_s, x_s, x_r, g_s, g_r, p_s, p_r, h_s, h_r,
):
    p = lax.axis_index("pipe")
    h = lax.axis_index("hidden")
    z, x = h // 4, lax.rem(h, 4)
    y, c = p // 2, lax.rem(p, 2)
    partner = p + 1 - 2 * c
    last = LAYERS - 1

    fac_in = pltpu.make_async_copy(factors, fac, lsem.at[0])
    cot_in = pltpu.make_async_copy(cot.at[pl.ds(pl.multiple_of(p * N, N), N)], gs.at[LAYERS], lsem.at[1])
    x_in = pltpu.make_async_copy(acts.at[pl.ds(pl.multiple_of(p * N, N), N)], xs.at[p], lsem.at[2])
    fac_in.start()
    cot_in.start()
    x_in.start()

    bar = pltpu.get_barrier_semaphore()

    def greet_hidden(k, _):
        pl.semaphore_signal(bar, inc=1, device_id={"hidden": lax.rem(h + k, PEERS)}, device_id_type=MESH)
        return 0

    def greet_pipe(k, _):
        pl.semaphore_signal(bar, inc=1, device_id={"pipe": lax.rem(p + k, LAYERS)}, device_id_type=MESH)
        return 0

    lax.fori_loop(1, PEERS, greet_hidden, 0)
    lax.fori_loop(1, LAYERS, greet_pipe, 0)

    fac_in.wait()

    def prepare(kind):
        if kind in (R1, R2):
            st[...] = fac[kind].astype(F32)
            for a in range(OWN):
                for cl in range(OWN):
                    rows = st[pl.ds(a * N + cl, N // OWN, stride=OWN), :]
                    wts[p, kind, pl.ds(a * N + cl * (N // OWN), N // OWN)] = rows.astype(BF)
        else:
            for b in range(OWN):
                wts[p, kind, blk(b)] = fac[kind, blk(b)].T

    for kind in (L2, R1, L1, R2):
        prepare(kind)
    pl.semaphore_wait(bar, PEERS - 1 + LAYERS - 1)

    def send_w(kind):
        for dest in (lax.rem(p + 2, LAYERS), lax.rem(p + 6, LAYERS), lax.rem(p + 4, LAYERS), partner):
            pltpu.make_async_remote_copy(
                src_ref=wts.at[p, kind], dst_ref=wts.at[p, kind], send_sem=w_s.at[kind], recv_sem=w_r.at[p, kind],
                device_id={"pipe": dest}, device_id_type=MESH,
            ).start()

    def send_x():
        def one(k, _):
            q = lax.rem(p + k, LAYERS)
            pltpu.make_async_remote_copy(
                src_ref=acts.at[pl.ds(pl.multiple_of(q * N, N), N)], dst_ref=xs.at[p], send_sem=x_s, recv_sem=x_r.at[p],
                device_id={"pipe": q}, device_id_type=MESH,
            ).start()
            return 0

        lax.fori_loop(1, LAYERS, one, 0)

    def fwd_copy(l, kind):
        return pltpu.make_async_remote_copy(
            src_ref=wts.at[l, kind], dst_ref=wts.at[l, kind], send_sem=f_s.at[l, kind], recv_sem=w_r.at[l, kind],
            device_id={"pipe": partner}, device_id_type=MESH,
        )

    def wait_w(l, kind):
        pltpu.make_async_copy(wts.at[l, kind], wts.at[l, kind], w_r.at[l, kind]).wait()

    def forward_w(l, kind):
        @pl.when(jnp.logical_and(lax.rem(l, 2) == c, l != p))
        def _():
            wait_w(l, kind)
            fwd_copy(l, kind).start()

    def need_w(l, kind):
        @pl.when(lax.rem(l, 2) != c)
        def _():
            wait_w(l, kind)

    def need_x(l):
        @pl.when(l == p)
        def _():
            x_in.wait()

        @pl.when(l != p)
        def _():
            pltpu.make_async_copy(xs.at[l], xs.at[l], x_r.at[l]).wait()

    def exchange(which, l):
        def one(k, _):
            i, j = k // 4, lax.rem(k, 4)
            hi, hj = (i + 1) // 2, (j + 1) // 2
            dz = 4 + hi * (1 - 2 * lax.rem(i, 2))
            dx = 2 + hj * (1 - 2 * lax.rem(j, 2))
            d = lax.rem(z + dz, 8) * 4 + lax.rem(x + dx, 4)
            pltpu.make_async_remote_copy(
                src_ref=send.at[which, l, pl.ds(pl.multiple_of(d * PIECE, PIECE), PIECE)],
                dst_ref=recv.at[which, l, pl.ds(pl.multiple_of(h * PIECE, PIECE), PIECE)],
                send_sem=a_s.at[which, l], recv_sem=a_r.at[which, l],
                device_id={"hidden": d}, device_id_type=MESH,
            ).start()
            return 0

        lax.fori_loop(0, PEERS - 1, one, 0)
        mine = pl.ds(pl.multiple_of(h * PIECE, PIECE), PIECE)
        recv[which, l, mine] = send[which, l, mine]

    def arrived(which, l):
        rows = recv.at[which, l, pl.ds(0, (PEERS - 1) * PIECE)]
        pltpu.make_async_copy(rows, rows, a_r.at[which, l]).wait()

    def produce_u(which, l, kind, value):
        for a in range(OWN):
            part = dot(wts[l, kind, blk(a)], value[:, a * N:(a + 1) * N], 1, 1)
            for cl in range(OWN):
                st[pl.ds(a * OWN + cl, PEERS, stride=PIECE), :] = part[cl * PEERS:(cl + 1) * PEERS]
        send[which, l] = st[...].astype(BF)
        exchange(which, l)

    def produce_d(which, l, kind, value):
        for b in range(OWN):
            st[pl.ds(b, N, stride=OWN), :] = dot(wts[l, kind, blk(b)], value[:, b * N:(b + 1) * N], 1, 1)
        send[which, l] = st[...].astype(BF)
        exchange(which, l)

    def take_u(which, l, out):
        arrived(which, l)
        st[...] = recv[which, l].astype(F32)
        for b in range(OWN):
            out[blk(b)] = st[pl.ds(b, N, stride=OWN), :].astype(BF)

    def take_d(which, l, out):
        arrived(which, l)
        st[...] = recv[which, l].astype(F32)
        for a in range(OWN):
            for cl in range(OWN):
                out[pl.ds(a * N + cl * PEERS, PEERS)] = st[pl.ds(a * OWN + cl, PEERS, stride=PIECE), :].astype(BF)

    def partial(l, kind, left, right):
        for b in range(OWN):
            pg[l, kind, blk(b)] = dot(left[blk(b)], right[:, blk(b)], 1, 0).astype(BF)

    def pair_copy(l, kind):
        return pltpu.make_async_remote_copy(
            src_ref=pg.at[l, kind, pl.ds(pl.multiple_of((1 - c) * HALF, HALF), HALF)], dst_ref=px.at[l, kind],
            send_sem=p_s.at[l, kind], recv_sem=p_r.at[l, kind], device_id={"pipe": partner}, device_id_type=MESH,
        )

    def home_copy(l, kind):
        return pltpu.make_async_remote_copy(
            src_ref=hs.at[l, kind], dst_ref=home.at[kind, p], send_sem=h_s.at[l, kind], recv_sem=h_r.at[kind],
            device_id={"pipe": l}, device_id_type=MESH,
        )

    def reduce(l, kind):
        pair_copy(l, kind).wait_recv()
        own = pg[l, kind, pl.ds(pl.multiple_of(c * HALF, HALF), HALF)]
        total = (own.astype(F32) + px[l, kind].astype(F32)).astype(BF)

        @pl.when(l == p)
        def _():
            home[kind, p] = total

        @pl.when(l != p)
        def _():
            hs[l, kind] = total
            home_copy(l, kind).start()

    def gin_copy(l):
        return pltpu.make_async_remote_copy(
            src_ref=gs.at[l], dst_ref=gin.at[pl.ds(pl.multiple_of(p * N, N), N)], send_sem=g_s.at[l], recv_sem=g_r,
            device_id={"pipe": l}, device_id_type=MESH,
        )

    def gin_own(l):
        return pltpu.make_async_copy(gs.at[l], gin.at[pl.ds(pl.multiple_of(p * N, N), N)], lsem.at[1])

    def first_half(l):
        need_w(l, R1)
        need_x(l)
        produce_u(U1, l, R1, xs[l])

    def second_half(l):
        slot = lax.rem(l, 2)
        need_w(l, L1)
        take_u(U1, l, vu1)
        coeff = 0.7978845608028654
        for b in range(OWN):
            v = dot(vu1[blk(b)], wts[l, L1, blk(b)], 0, 0)
            tangent = jnp.tanh(coeff * (v + 0.044715 * (v * v * v)))
            act[:, b * N:(b + 1) * N] = (0.5 * v * (1.0 + tangent)).astype(BF)
            slope[:, b * N:(b + 1) * N] = 0.5 * (1.0 + tangent) + 0.5 * v * (1.0 - tangent * tangent) * coeff * (
                1.0 + 3.0 * 0.044715 * v * v
            )
        need_w(l, R2)
        produce_u(U2, l, R2, act[...])

    @pl.when(p == last)
    def _():
        send_w(L2)
        send_w(R1)
        send_x()
        send_w(L1)
        send_w(R2)

    cot_in.wait()
    forward_w(last, L2)

    def step(s, _):
        l = last - s
        need_w(l, L2)
        produce_d(D2, l, L2, gs[l + 1])

        @pl.when(s == 0)
        def _():
            forward_w(last, R1)
            first_half(last)
            forward_w(last, L1)
            forward_w(last, R2)

        second_half(l)

        @pl.when(jnp.logical_and(s == 0, p == last - 1))
        def _():
            send_w(R1)
            send_x()
            send_w(L2)
            send_w(L1)
            send_w(R2)

        @pl.when(s > 0)
        def _():
            partial(l + 1, R1, vd1, xs.at[l + 1])
            pair_copy(l + 1, R1).start()
            reduce(l + 1, R2)
            reduce(l + 1, L1)
            reduce(l + 1, L2)

            @pl.when(s < last)
            def _():
                forward_w(l - 1, R1)
                forward_w(l - 1, L2)

        take_d(D2, l, vd2)
        for b in range(OWN):
            da = dot(vd2[blk(b)], wts[l, R2, blk(b)], 0, 0)
            dh[:, b * N:(b + 1) * N] = (da * slope[:, b * N:(b + 1) * N]).astype(BF)
        produce_d(D1, l, L1, dh[...])

        @pl.when(p == 5 - s)
        def _():
            send_w(R1)
            send_w(L2)
            send_x()
            send_w(L1)
            send_w(R2)

        partial(l, R2, vd2, act)
        pair_copy(l, R2).start()
        partial(l, L1, vu1, dh)
        pair_copy(l, L1).start()
        take_u(U2, l, vu2)
        partial(l, L2, vu2, gs.at[l + 1])
        pair_copy(l, L2).start()

        @pl.when(s > 0)
        def _():
            reduce(l + 1, R1)

        @pl.when(s < last)
        def _():
            @pl.when(s == 0)
            def _():
                forward_w(l - 1, R1)
                forward_w(l - 1, L2)

            first_half(l - 1)
            forward_w(l - 1, L1)
            forward_w(l - 1, R2)

        take_d(D1, l, vd1)
        for b in range(OWN):
            dx = dot(vd1[blk(b)], wts[l, R1, blk(b)], 0, 0)
            gs[l, :, b * N:(b + 1) * N] = (gs[l + 1, :, b * N:(b + 1) * N].astype(F32) + dx).astype(BF)

        @pl.when(l == p)
        def _():
            gin_own(l).start()

        @pl.when(l != p)
        def _():
            gin_copy(l).start()

        return 0

    lax.fori_loop(0, LAYERS, step, 0)

    partial(0, R1, vd1, xs.at[0])
    pair_copy(0, R1).start()
    reduce(0, R2)
    reduce(0, L1)
    reduce(0, L2)
    reduce(0, R1)

    def finish(kind):
        seven = home.at[kind, pl.ds(0, LAYERS - 1)]
        pltpu.make_async_copy(seven, seven, h_r.at[kind]).wait()
        for half in range(2):
            total = home[kind, half].astype(F32)
            for group in range(1, LAYERS // 2):
                total = total + home[kind, 2 * group + half].astype(F32)
            total = total * (LAYERS * N) ** -0.5
            for b in range(2):
                i = half * 2 + b
                own = total[b * N:(b + 1) * N]
                if kind in (R1, R2):
                    for cl in range(OWN):
                        fin[kind, pl.ds(i * N + cl, PEERS, stride=OWN), :] = own[cl * PEERS:(cl + 1) * PEERS]
                else:
                    fin[kind, blk(i)] = own.T
        out = pltpu.make_async_copy(fin.at[kind], gfac.at[kind], lsem.at[3 + kind])
        out.start()
        return out

    outs = [finish(kind) for kind in (R2, L1, L2, R1)]
    for out in outs:
        out.wait()

    seven = gin.at[pl.ds(0, (LAYERS - 1) * N)]
    pltpu.make_async_copy(seven, seven, g_r).wait()
    gin_own(p).wait()

    def drain(l, _):
        for which in range(4):
            rows = send.at[which, l, pl.ds(0, (PEERS - 1) * PIECE)]
            pltpu.make_async_copy(rows, rows, a_s.at[which, l]).wait()
        for kind in range(4):
            pair_copy(l, kind).wait_send()

            @pl.when(l != p)
            def _():
                home_copy(l, kind).wait_send()

            @pl.when(jnp.logical_and(lax.rem(l, 2) == c, l != p))
            def _():
                fwd_copy(l, kind).wait_send()

        @pl.when(l != p)
        def _():
            gin_copy(l).wait_send()

        return 0

    lax.fori_loop(0, LAYERS, drain, 0)
    for kind in range(4):
        four = wts.at[p, pl.ds(0, 4)]
        pltpu.make_async_copy(four, four, w_s.at[kind]).wait()
    pltpu.make_async_copy(seven, seven, x_s).wait()


def shards(acts, factors, cotangent):
    dma = pltpu.SemaphoreType.DMA
    gin, gfac = pl.pallas_call(
        kernel,
        name="monarch_backward",
        out_shape=(
            jax.ShapeDtypeStruct((LAYERS * N, FEAT), BF),
            jax.ShapeDtypeStruct((4, FEAT, N), F32),
        ),
        in_specs=[pl.BlockSpec(memory_space=pl.ANY)] * 3,
        out_specs=(pl.BlockSpec(memory_space=pl.ANY), pl.BlockSpec(memory_space=pl.ANY)),
        scratch_shapes=[
            pltpu.VMEM((4, FEAT, N), BF),
            pltpu.VMEM((LAYERS, 4, FEAT, N), BF),
            pltpu.VMEM((LAYERS, N, FEAT), BF),
            pltpu.VMEM((LAYERS + 1, N, FEAT), BF),
            pltpu.VMEM((4, LAYERS, FEAT, N), BF),
            pltpu.VMEM((4, LAYERS, FEAT, N), BF),
            pltpu.VMEM((FEAT, N), F32),
            pltpu.VMEM((FEAT, N), BF),
            pltpu.VMEM((FEAT, N), BF),
            pltpu.VMEM((FEAT, N), BF),
            pltpu.VMEM((FEAT, N), BF),
            pltpu.VMEM((N, FEAT), BF),
            pltpu.VMEM((N, FEAT), F32),
            pltpu.VMEM((N, FEAT), BF),
            pltpu.VMEM((LAYERS, 4, FEAT, N), BF),
            pltpu.VMEM((LAYERS, 4, HALF, N), BF),
            pltpu.VMEM((LAYERS, 4, HALF, N), BF),
            pltpu.VMEM((4, LAYERS, HALF, N), BF),
            pltpu.VMEM((4, FEAT, N), F32),
            dma((7,)),
            dma((4, LAYERS)), dma((4, LAYERS)),
            dma((4,)), dma((LAYERS, 4)), dma((LAYERS, 4)),
            dma, dma((LAYERS,)),
            dma((LAYERS,)), dma,
            dma((LAYERS, 4)), dma((LAYERS, 4)),
            dma((LAYERS, 4)), dma((4,)),
        ],
        compiler_params=pltpu.CompilerParams(
            collective_id=0, has_side_effects=True, vmem_limit_bytes=48 * 2**20
        ),
    )(acts.reshape(LAYERS * N, FEAT), factors.reshape(4, FEAT, N), cotangent)
    return gin.reshape(1, LAYERS * N, FEAT), gfac.reshape(1, 4, OWN, N, N)


def solution(mesh):
    in_specs = (P("pipe", None, "hidden"), P("pipe", None, "hidden", None, None), P(None, "hidden"))
    out_specs = (P("pipe", None, "hidden"), P("pipe", None, "hidden", None, None))
    return jax.shard_map(shards, mesh=mesh, in_specs=in_specs, out_specs=out_specs, check_vma=False)
```

time: 690 us -> 187 us (0.27); the launches traced: 681 us -> 187 us
  waiting for transfers between devices: 274 us -> 0 us
  starting transfers between devices: 189 us -> 0 us
  Pallas kernels: 0 us -> 181 us
  local copies, waits for them, and re-layouts: 97.5 us -> 5.43 us
  matrix products: 70.8 us -> 0 us
  blocking collectives: 39.5 us -> 0 us
  other arithmetic: 7.06 us -> 0 us
    all_to_all x31 -> x0, waiting for transfers between devices: 239 us -> none  [the longest x30 214 us: advance(): lax.all_to_all(sent, 'hidden', split_axis=0, concat_axis=1, tiled=True)]
    pallas_call x0 -> x1, Pallas kernels: none -> 181 us  [shards(): pl.pallas_call(kernel, name='monarch_backward', out_shape=(jax.ShapeDtype...]
    all_to_all x31 -> x0, starting transfers between devices: 169 us -> none  [the longest x30 164 us: advance(): lax.all_to_all(sent, 'hidden', split_axis=0, concat_axis=1, tiled=True)]
    dot_general x123 -> x0, matrix products: 70.8 us -> none  [the longest x30 32.9 us: grad_pair(): jnp.einsum('act,tab->acb', grad_part, inputs, preferred_element_type=jnp....]
    dynamic_slice x60 -> x0, local copies, waits for them, and re-layouts: 46.2 us -> none  [the longest x15 16.1 us: advance(): mixed_two = lax.dynamic_slice_in_dim(stored[3], start, piece_rows, 2)]
    all_to_all x1 -> x0, blocking collectives: 39.5 us -> none  [shards(): lax.all_to_all(sent, 'hidden', split_axis=1, concat_axis=0, tiled=True)]
    ppermute x15 -> x0, waiting for transfers between devices: 34.9 us -> none  [shifted(): lax.ppermute(value, axis, [(source, source + steps) for source in range(l...]
    convert_element_type x32 -> x0, local copies, waits for them, and re-layouts: 25.7 us -> none  [the longest x30 23.2 us: grad_pair(): mixed_gradient = jnp.einsum('tcd,cda->act', grad_out, left_factor, prefer...]
  transfers between devices with their start and end apart: 46 -> 0, of which waited for: 46 -> 0; matrix products, arithmetic and copies ran while one was open for 11% -> 0% of each run, Pallas kernels for 0% -> 0%
where the time goes in v1:
time: 187 us
  Pallas kernels  181 us (97%)
  local copies, waits for them, and re-layouts  5.43 us (3%)
    pallas_call x1, Pallas kernels, shards(): pl.pallas_call(kernel, name='monarch_backward', out_shape=(jax.ShapeDtype...  181 us
    unnamed x8, local copies, waits for them, and re-layouts  5.43 us

profile of v1, /device:TPU:2, one launch (start us, length us, event | category | flops | bytes accessed | tf_op | source)
XLA Modules:
  0.0 186.9 jit_solution(7939144410419461883)
XLA Ops:
  0.6 0.0 copy-start
  0.6 1.2 copy-done
  1.9 0.0 copy-start.1
  1.9 1.2 copy-done.1
  3.1 0.0 copy-start.2
  3.1 1.0 copy-done.2
  4.1 180.8 %monarch_backward.1 = (bf16[1024,512]{1,0:T(8,128)(2,1)S(1)}, f32[4,512,128]{2,1,0:T(8,128)S(1)}) custom-call(bf16[1024,512]{1,0:T(8,128)(2,1)S(1)} %bitcast.4, bf16[4,512,128]{2,1,0:T(8,128)(2,1)S(1)} %bitcast.7, bf16[1024,512]{1,0:T(8,128)(2,1)S(1)} %copy-done.1), custom_call_target="tpu_custom_call" | custom-call | tf_op jit(solution)/shard_map/monarch_backward/pallas_call | solution.py:400
  184.9 1.0 copy.7
  185.9 1.0 copy.8
Async XLA Ops:
  0.6 1.2 copy-start
  1.9 1.2 copy-start.1
  3.1 1.0 copy-start.2

commit v2 on v1

--- a/solution.py
+++ b/solution.py
@@ -152,7 +152,6 @@
             for cl in range(OWN):
                 st[pl.ds(a * OWN + cl, PEERS, stride=PIECE), :] = part[cl * PEERS:(cl + 1) * PEERS]
         send[which, l] = st[...].astype(BF)
-        exchange(which, l)
 
     def produce_d(which, l, kind, value):
         for b in range(OWN):
@@ -220,62 +219,82 @@
     def second_half(l):
         slot = lax.rem(l, 2)
         need_w(l, L1)
-        take_u(U1, l, vu1)
+        take_u(U1, l, vu1.at[slot])
         coeff = 0.7978845608028654
         for b in range(OWN):
-            v = dot(vu1[blk(b)], wts[l, L1, blk(b)], 0, 0)
+            v = dot(vu1[slot, blk(b)], wts[l, L1, blk(b)], 0, 0)
             tangent = jnp.tanh(coeff * (v + 0.044715 * (v * v * v)))
-            act[:, b * N:(b + 1) * N] = (0.5 * v * (1.0 + tangent)).astype(BF)
+            act[slot, :, b * N:(b + 1) * N] = (0.5 * v * (1.0 + tangent)).astype(BF)
             slope[:, b * N:(b + 1) * N] = 0.5 * (1.0 + tangent) + 0.5 * v * (1.0 - tangent * tangent) * coeff * (
                 1.0 + 3.0 * 0.044715 * v * v
             )
         need_w(l, R2)
-        produce_u(U2, l, R2, act[...])
-
-    @pl.when(p == last)
-    def _():
+        produce_u(U2, l, R2, act[slot])
+
+    def send_all():
         send_w(L2)
         send_w(R1)
         send_x()
         send_w(L1)
         send_w(R2)
 
+    @pl.when(p == last)
+    def _():
+        send_all()
+
     cot_in.wait()
     forward_w(last, L2)
 
     def step(s, _):
         l = last - s
+        slot = lax.rem(l, 2)
         need_w(l, L2)
         produce_d(D2, l, L2, gs[l + 1])
 
+        @pl.when(jnp.logical_and(s >= 2, l >= 1))
+        def _():
+            exchange(U1, l - 1)
+
+        @pl.when(l == 0)
+        def _():
+            exchange(U2, l)
+
         @pl.when(s == 0)
         def _():
-            forward_w(last, R1)
-            first_half(last)
-            forward_w(last, L1)
-            forward_w(last, R2)
-
-        second_half(l)
-
-        @pl.when(jnp.logical_and(s == 0, p == last - 1))
-        def _():
-            send_w(R1)
-            send_x()
-            send_w(L2)
-            send_w(L1)
-            send_w(R2)
-
-        @pl.when(s > 0)
+            pl.when(p == 5)(send_all)
+            forward_w(l, R1)
+            first_half(l)
+            exchange(U1, l)
+            pl.when(jnp.logical_or(p == 6, p < 5))(send_all)
+            forward_w(l, L1)
+            forward_w(l, R2)
+
+        @pl.when(s <= 1)
+        def _():
+            second_half(l)
+
+        @pl.when(s == 1)
+        def _():
+            forward_w(l - 1, R1)
+            first_half(l - 1)
+            exchange(U1, l - 1)
+
+        @pl.when(s >= 1)
         def _():
             partial(l + 1, R1, vd1, xs.at[l + 1])
             pair_copy(l + 1, R1).start()
-            reduce(l + 1, R2)
-            reduce(l + 1, L1)
-            reduce(l + 1, L2)
-
-            @pl.when(s < last)
+            take_u(U2, l + 1, vu2)
+            partial(l + 1, L2, vu2, gs.at[l + 2])
+            pair_copy(l + 1, L2).start()
+
+            @pl.when(l >= 2)
             def _():
-                forward_w(l - 1, R1)
+                forward_w(l - 2, R1)
+
+            @pl.when(l >= 1)
+            def _():
+                forward_w(l - 1, L1)
+                forward_w(l - 1, R2)
                 forward_w(l - 1, L2)
 
         take_d(D2, l, vd2)
@@ -284,36 +303,52 @@
             dh[:, b * N:(b + 1) * N] = (da * slope[:, b * N:(b + 1) * N]).astype(BF)
         produce_d(D1, l, L1, dh[...])
 
-        @pl.when(p == 5 - s)
-        def _():
-            send_w(R1)
-            send_w(L2)
-            send_x()
-            send_w(L1)
-            send_w(R2)
-
-        partial(l, R2, vd2, act)
+        @pl.when(l >= 1)
+        def _():
+            exchange(U2, l)
+
+        @pl.when(s == 0)
+        def _():
+            forward_w(l - 1, R1)
+            first_half(l - 1)
+            exchange(U1, l - 1)
+
+        partial(l, R2, vd2, act.at[slot])
         pair_copy(l, R2).start()
-        partial(l, L1, vu1, dh)
+        partial(l, L1, vu1.at[slot], dh)
         pair_copy(l, L1).start()
-        take_u(U2, l, vu2)
-        partial(l, L2, vu2, gs.at[l + 1])
-        pair_copy(l, L2).start()
-
-        @pl.when(s > 0)
-        def _():
-            reduce(l + 1, R1)
-
-        @pl.when(s < last)
-        def _():
-            @pl.when(s == 0)
-            def _():
-                forward_w(l - 1, R1)
-                forward_w(l - 1, L2)
-
-            first_half(l - 1)
+
+        @pl.when(jnp.logical_and(s >= 1, l >= 1))
+        def _():
+            second_half(l - 1)
+
+        @pl.when(jnp.logical_and(s >= 1, l >= 2))
+        def _():
+            first_half(l - 2)
+
+        @pl.when(s == 0)
+        def _():
             forward_w(l - 1, L1)
             forward_w(l - 1, R2)
+            forward_w(l - 1, L2)
+
+        @pl.when(s >= 1)
+        def _():
+            reduce(l + 1, R1)
+            reduce(l + 1, L2)
+
+        @pl.when(l == 0)
+        def _():
+            take_u(U2, l, vu2)
+            partial(l, L2, vu2, gs.at[l + 1])
+            pair_copy(l, L2).start()
+
+        reduce(l, R2)
+        reduce(l, L1)
+
+        @pl.when(l == 0)
+        def _():
+            reduce(l, L2)
 
         take_d(D1, l, vd1)
         for b in range(OWN):
@@ -334,9 +369,6 @@
 
     partial(0, R1, vd1, xs.at[0])
     pair_copy(0, R1).start()
-    reduce(0, R2)
-    reduce(0, L1)
-    reduce(0, L2)
     reduce(0, R1)
 
     def finish(kind):
@@ -414,11 +446,11 @@
             pltpu.VMEM((4, LAYERS, FEAT, N), BF),
             pltpu.VMEM((4, LAYERS, FEAT, N), BF),
             pltpu.VMEM((FEAT, N), F32),
+            pltpu.VMEM((2, FEAT, N), BF),
             pltpu.VMEM((FEAT, N), BF),
             pltpu.VMEM((FEAT, N), BF),
             pltpu.VMEM((FEAT, N), BF),
-            pltpu.VMEM((FEAT, N), BF),
-            pltpu.VMEM((N, FEAT), BF),
+            pltpu.VMEM((2, N, FEAT), BF),
             pltpu.VMEM((N, FEAT), F32),
             pltpu.VMEM((N, FEAT), BF),
             pltpu.VMEM((LAYERS, 4, FEAT, N), BF),
@@ -435,7 +467,7 @@
             dma((LAYERS, 4)), dma((4,)),
         ],
         compiler_params=pltpu.CompilerParams(
-            collective_id=0, has_side_effects=True, vmem_limit_bytes=48 * 2**20
+            collective_id=0, has_side_effects=True, vmem_limit_bytes=63 * 2**20
         ),
     )(acts.reshape(LAYERS * N, FEAT), factors.reshape(4, FEAT, N), cotangent)
     return gin.reshape(1, LAYERS * N, FEAT), gfac.reshape(1, 4, OWN, N, N)

time: 187 us -> 160 us (0.86)
  Pallas kernels: 181 us -> 156 us
  local copies, waits for them, and re-layouts: 5.43 us -> 3.32 us
    pallas_call x1, Pallas kernels: 181 us -> 156 us  [shards(): pl.pallas_call(kernel, name='monarch_backward', out_shape=(jax.ShapeDtype...]
    unnamed x8 -> x4, local copies, waits for them, and re-layouts: 5.43 us -> 3.32 us
where the time goes in v2:
time: 160 us
  Pallas kernels  156 us (98%)
  local copies, waits for them, and re-layouts  3.32 us (2%)
    pallas_call x1, Pallas kernels, shards(): pl.pallas_call(kernel, name='monarch_backward', out_shape=(jax.ShapeDtype...  156 us
    unnamed x4, local copies, waits for them, and re-layouts  3.32 us

profile of v2, /device:TPU:2, one launch (start us, length us, event | category | flops | bytes accessed | tf_op | source)
XLA Modules:
  0.0 159.9 jit_solution(10752150431278308256)
XLA Ops:
  0.6 155.9 %monarch_backward.1 = (bf16[1024,512]{1,0:T(8,128)(2,1)}, f32[4,512,128]{2,1,0:T(8,128)}) custom-call(bf16[1024,512]{1,0:T(8,128)(2,1)} %bitcast.4, bf16[4,512,128]{2,1,0:T(8,128)(2,1)} %bitcast.7, bf16[1024,512]{1,0:T(8,128)(2,1)} %cot.1), custom_call_target="tpu_custom_call" | custom-call | tf_op jit(solution)/shard_map/monarch_backward/pallas_call | solution.py:432
  156.5 0.0 copy-start
  156.5 2.4 %copy.7 = bf16[1,1024,512]{2,1,0:T(8,128)(2,1)} copy(bf16[1,1024,512]{2,1,0:T(8,128)(2,1)} %bitcast.6) | data formatting | bytes 2097152
  158.9 0.0 copy-done
  158.9 1.0 copy.8
Async XLA Ops:
  156.5 2.4 %copy-start = (f32[4,512,128]{2,1,0:T(8,128)S(1)}, f32[4,512,128]{2,1,0:T(8,128)}, u32[]{:S(2)}) copy-start(f32[4,512,128]{2,1,0:T(8,128)} %get-tuple-element.5) | copy-start | bytes 3145732

commit v3 on v2

--- a/solution.py
+++ b/solution.py
@@ -17,6 +17,8 @@
 R1, L1, R2, L2 = 0, 1, 2, 3
 U1, U2, D1, D2 = 0, 1, 2, 3
 HALF = FEAT // 2
+EARLY = 6
+RELAYED = (R1, L1, R2,)
 
 
 def dot(a, b, ca, cb):
@@ -30,7 +32,7 @@
 def kernel(
     acts, factors, cot, gin, gfac,
     fac, wts, xs, gs, send, recv, st, vu1, vd2, vd1, vu2, act, slope, dh, pg, px, hs, home, fin,
-    lsem, a_s, a_r, w_s, w_r, f_s, x_s, x_r, g_s, g_r, p_s, p_r, h_s, h_r,
+    lsem, a_s, a_r, w_s, w_r, f_s, y_s, x_s, x_r, g_s, g_r, p_s, p_r, h_s, h_r,
 ):
     p = lax.axis_index("pipe")
     h = lax.axis_index("hidden")
@@ -77,11 +79,19 @@
     pl.semaphore_wait(bar, PEERS - 1 + LAYERS - 1)
 
     def send_w(kind):
-        for dest in (lax.rem(p + 2, LAYERS), lax.rem(p + 6, LAYERS), lax.rem(p + 4, LAYERS), partner):
+        def to(dest):
             pltpu.make_async_remote_copy(
                 src_ref=wts.at[p, kind], dst_ref=wts.at[p, kind], send_sem=w_s.at[kind], recv_sem=w_r.at[p, kind],
                 device_id={"pipe": dest}, device_id_type=MESH,
             ).start()
+
+        to(lax.rem(p + 2, LAYERS))
+        to(lax.rem(p + 6, LAYERS))
+        if kind in RELAYED:
+            pl.when(p < EARLY)(lambda: to(lax.rem(p + 4, LAYERS)))
+        else:
+            to(lax.rem(p + 4, LAYERS))
+        to(partner)
 
     def send_x():
         def one(k, _):
@@ -100,6 +110,15 @@
             device_id={"pipe": partner}, device_id_type=MESH,
         )
 
+    def relay_copy(l, kind):
+        return pltpu.make_async_remote_copy(
+            src_ref=wts.at[l, kind], dst_ref=wts.at[l, kind], send_sem=y_s.at[l, kind], recv_sem=w_r.at[l, kind],
+            device_id={"pipe": lax.rem(l + 4, LAYERS)}, device_id_type=MESH,
+        )
+
+    def relays(l):
+        return jnp.logical_and(l >= EARLY, p == lax.rem(l + 6, LAYERS))
+
     def wait_w(l, kind):
         pltpu.make_async_copy(wts.at[l, kind], wts.at[l, kind], w_r.at[l, kind]).wait()
 
@@ -107,6 +126,8 @@
         @pl.when(jnp.logical_and(lax.rem(l, 2) == c, l != p))
         def _():
             wait_w(l, kind)
+            if kind in RELAYED:
+                pl.when(relays(l))(lambda: relay_copy(l, kind).start())
             fwd_copy(l, kind).start()
 
     def need_w(l, kind):
@@ -255,10 +276,6 @@
         def _():
             exchange(U1, l - 1)
 
-        @pl.when(l == 0)
-        def _():
-            exchange(U2, l)
-
         @pl.when(s == 0)
         def _():
             pl.when(p == 5)(send_all)
@@ -297,6 +314,12 @@
                 forward_w(l - 1, R2)
                 forward_w(l - 1, L2)
 
+        @pl.when(l == 0)
+        def _():
+            take_u(U2, l, vu2)
+            partial(l, L2, vu2, gs.at[l + 1])
+            pair_copy(l, L2).start()
+
         take_d(D2, l, vd2)
         for b in range(OWN):
             da = dot(vd2[blk(b)], wts[l, R2, blk(b)], 0, 0)
@@ -326,6 +349,10 @@
         def _():
             first_half(l - 2)
 
+        @pl.when(l == 1)
+        def _():
+            exchange(U2, l - 1)
+
         @pl.when(s == 0)
         def _():
             forward_w(l - 1, L1)
@@ -337,20 +364,18 @@
             reduce(l + 1, R1)
             reduce(l + 1, L2)
 
-        @pl.when(l == 0)
-        def _():
-            take_u(U2, l, vu2)
-            partial(l, L2, vu2, gs.at[l + 1])
-            pair_copy(l, L2).start()
+        pl.when(l == 0)(lambda: reduce(l, L2))
 
         reduce(l, R2)
         reduce(l, L1)
 
+        take_d(D1, l, vd1)
+
         @pl.when(l == 0)
         def _():
-            reduce(l, L2)
-
-        take_d(D1, l, vd1)
+            partial(l, R1, vd1, xs.at[l])
+            pair_copy(l, R1).start()
+
         for b in range(OWN):
             dx = dot(vd1[blk(b)], wts[l, R1, blk(b)], 0, 0)
             gs[l, :, b * N:(b + 1) * N] = (gs[l + 1, :, b * N:(b + 1) * N].astype(F32) + dx).astype(BF)
@@ -367,8 +392,6 @@
 
     lax.fori_loop(0, LAYERS, step, 0)
 
-    partial(0, R1, vd1, xs.at[0])
-    pair_copy(0, R1).start()
     reduce(0, R1)
 
     def finish(kind):
@@ -413,6 +436,8 @@
             @pl.when(jnp.logical_and(lax.rem(l, 2) == c, l != p))
             def _():
                 fwd_copy(l, kind).wait_send()
+                if kind in RELAYED:
+                    pl.when(relays(l))(lambda: relay_copy(l, kind).wait_send())
 
         @pl.when(l != p)
         def _():
@@ -421,9 +446,16 @@
         return 0
 
     lax.fori_loop(0, LAYERS, drain, 0)
+    def sent(kind, copies):
+        part = wts.at[p, pl.ds(0, copies)]
+        pltpu.make_async_copy(part, part, w_s.at[kind]).wait()
+
     for kind in range(4):
-        four = wts.at[p, pl.ds(0, 4)]
-        pltpu.make_async_copy(four, four, w_s.at[kind]).wait()
+        if kind in RELAYED:
+            pl.when(p < EARLY)(lambda: sent(kind, 4))
+            pl.when(p >= EARLY)(lambda: sent(kind, 3))
+        else:
+            sent(kind, 4)
     pltpu.make_async_copy(seven, seven, x_s).wait()
 
 
@@ -460,7 +492,7 @@
             pltpu.VMEM((4, FEAT, N), F32),
             dma((7,)),
             dma((4, LAYERS)), dma((4, LAYERS)),
-            dma((4,)), dma((LAYERS, 4)), dma((LAYERS, 4)),
+            dma((4,)), dma((LAYERS, 4)), dma((LAYERS, 4)), dma((LAYERS, 4)),
             dma, dma((LAYERS,)),
             dma((LAYERS,)), dma,
             dma((LAYERS, 4)), dma((LAYERS, 4)),

time: 160 us -> 162 us (1.012)
  Pallas kernels: 156 us -> 158 us
    pallas_call x1, Pallas kernels: 156 us -> 158 us  [shards(): pl.pallas_call(kernel, name='monarch_backward', out_shape=(jax.ShapeDtype...]
where the time goes in v3:
time: 162 us
  Pallas kernels  158 us (98%)
  local copies, waits for them, and re-layouts  3.32 us (2%)
    pallas_call x1, Pallas kernels, shards(): pl.pallas_call(kernel, name='monarch_backward', out_shape=(jax.ShapeDtype...  158 us
    unnamed x4, local copies, waits for them, and re-layouts  3.32 us

profile of v3, /device:TPU:2, one launch (start us, length us, event | category | flops | bytes accessed | tf_op | source)
XLA Modules:
  0.0 162.2 jit_solution(15199644464342785150)
XLA Ops:
  0.6 158.2 %monarch_backward.1 = (bf16[1024,512]{1,0:T(8,128)(2,1)}, f32[4,512,128]{2,1,0:T(8,128)}) custom-call(bf16[1024,512]{1,0:T(8,128)(2,1)} %bitcast.4, bf16[4,512,128]{2,1,0:T(8,128)(2,1)} %bitcast.7, bf16[1024,512]{1,0:T(8,128)(2,1)} %cot.1), custom_call_target="tpu_custom_call" | custom-call | tf_op jit(solution)/shard_map/monarch_backward/pallas_call | solution.py:464
  158.9 0.0 copy-start
  158.9 2.4 %copy.7 = bf16[1,1024,512]{2,1,0:T(8,128)(2,1)} copy(bf16[1,1024,512]{2,1,0:T(8,128)(2,1)} %bitcast.6) | data formatting | bytes 2097152
  161.2 0.0 copy-done
  161.2 1.0 copy.8
Async XLA Ops:
  158.9 2.4 %copy-start = (f32[4,512,128]{2,1,0:T(8,128)S(1)}, f32[4,512,128]{2,1,0:T(8,128)}, u32[]{:S(2)}) copy-start(f32[4,512,128]{2,1,0:T(8,128)} %get-tuple-element.5) | copy-start | bytes 3145732

commit v4 on v3

--- a/solution.py
+++ b/solution.py
@@ -159,7 +159,7 @@
             ).start()
             return 0
 
-        lax.fori_loop(0, PEERS - 1, one, 0)
+        lax.fori_loop(0, PEERS - 1, one, 0, unroll=True)
         mine = pl.ds(pl.multiple_of(h * PIECE, PIECE), PIECE)
         recv[which, l, mine] = send[which, l, mine]
 

time: 162 us -> 158 us (0.975)
  Pallas kernels: 158 us -> 154 us
    pallas_call x1, Pallas kernels: 158 us -> 154 us  [shards(): pl.pallas_call(kernel, name='monarch_backward', out_shape=(jax.ShapeDtype...]
where the time goes in v4:
time: 158 us
  Pallas kernels  154 us (97%)
  local copies, waits for them, and re-layouts  3.32 us (2%)
    pallas_call x1, Pallas kernels, shards(): pl.pallas_call(kernel, name='monarch_backward', out_shape=(jax.ShapeDtype...  154 us
    unnamed x4, local copies, waits for them, and re-layouts  3.32 us

profile of v4, /device:TPU:2, one launch (start us, length us, event | category | flops | bytes accessed | tf_op | source)
XLA Modules:
  0.0 157.6 jit_solution(13941044876000692883)
XLA Ops:
  0.6 153.7 %monarch_backward.1 = (bf16[1024,512]{1,0:T(8,128)(2,1)}, f32[4,512,128]{2,1,0:T(8,128)}) custom-call(bf16[1024,512]{1,0:T(8,128)(2,1)} %bitcast.4, bf16[4,512,128]{2,1,0:T(8,128)(2,1)} %bitcast.7, bf16[1024,512]{1,0:T(8,128)(2,1)} %cot.1), custom_call_target="tpu_custom_call" | custom-call | tf_op jit(solution)/shard_map/monarch_backward/pallas_call | solution.py:464
  154.3 0.0 copy-start
  154.3 2.4 %copy.7 = bf16[1,1024,512]{2,1,0:T(8,128)(2,1)} copy(bf16[1,1024,512]{2,1,0:T(8,128)(2,1)} %bitcast.6) | data formatting | bytes 2097152
  156.7 0.0 copy-done
  156.7 1.0 copy.8
Async XLA Ops:
  154.3 2.4 %copy-start = (f32[4,512,128]{2,1,0:T(8,128)S(1)}, f32[4,512,128]{2,1,0:T(8,128)}, u32[]{:S(2)}) copy-start(f32[4,512,128]{2,1,0:T(8,128)} %get-tuple-element.5) | copy-start | bytes 3145732
